TPU v7x, 256 devices: a whole 4x4x8 slice. The times are simulated.
256 devices in a mesh: dp: 32 (over y, x, core), tensor: 8 (over z).
Axes of the slice: x: 4, y: 4, z: 8, core: 2. Of those that a mesh axis runs over, the one named last changes fastest.
Arguments:
- tokens: bfloat16 [16384, 5120], P(('dp', 'tensor')), may hold values from -6 to 6
- token_grads: bfloat16 [16384, 3072], P('dp', 'tensor'), may hold values from -0.625 to 0.625
- weight: bfloat16 [5120, 3072], P(None, 'tensor'), may hold values from -6 to 6
- feedback: bfloat16 [32, 5120, 3072], P('dp', None, 'tensor'), may hold values from -6 to 6
- q_start: float32 [3072, 32], P('tensor'), may hold values from -6 to 6
Outputs:
- input_grads: bfloat16 [16384, 5120], P(('dp', 'tensor'))
- new_feedback: bfloat16 [32, 5120, 3072], P('dp', None, 'tensor')
- q_next: float32 [3072, 32], P('tensor')
All inputs are finite; a program needn't handle non-finite values.
Results may differ from a plain program's by a relative error of at most 0.019.
Values may be sent and summed in bfloat16 or wider, within the bound.
A program may use at most 128 MiB of HBM per device.

v0:
```python
import jax
import jax.numpy as jnp
from jax import lax
from jax.sharding import PartitionSpec as P


def lower_solve(factor_low, columns):
    return jax.scipy.linalg.solve_triangular(factor_low, columns.T, lower=True).T


def local(tokens, token_grads, weight, feedback, q_start):
    n_tensor = lax.axis_size("tensor")
    n_replicas = lax.axis_size("dp")
    share = token_grads.shape[0] // n_tensor
    rows = token_grads
    every_row = lax.psum(
        lax.dot_general(
            rows, weight, (((1,), (1,)), ((), ())), preferred_element_type=jnp.float32
        ).astype(jnp.bfloat16),
        "tensor",
    ).astype(jnp.float32)
    own_start = lax.axis_index("tensor") * share
    input_grads = lax.dynamic_slice_in_dim(every_row, own_start, share, 0).astype(jnp.bfloat16)
    carried = feedback[0].astype(jnp.float32)
    rows = token_grads
    gradient = lax.dot_general(
        lax.all_gather(tokens, "tensor", axis=0, tiled=True),
        rows,
        (((0,), (0,)), ((), ())),
        preferred_element_type=jnp.float32,
    )
    merged = gradient + carried
    p_terms = jnp.dot(merged, q_start, precision=lax.Precision.HIGHEST)
    p_sum = lax.psum(p_terms, ("dp", "tensor"))
    gram_matrix = jnp.dot(p_sum.T, p_sum, precision=lax.Precision.HIGHEST)
    p_hat = lower_solve(jnp.linalg.cholesky(gram_matrix), p_sum)
    local_q = lax.dot_general(
        merged, p_hat, (((0,), (0,)), ((), ())), precision=lax.Precision.HIGHEST
    )
    q_next = lax.psum(local_q.astype(jnp.bfloat16), "dp").astype(jnp.float32) / n_replicas
    decompressed = jnp.dot(p_hat, q_next.T, precision=lax.Precision.HIGHEST)
    new_feedback = (merged - decompressed).astype(jnp.bfloat16)[None]
    return (input_grads, new_feedback, q_next)


def solution(mesh):
    return jax.shard_map(
        local,
        mesh=mesh,
        in_specs=(
            P(("dp", "tensor"), None),
            P("dp", "tensor"),
            P(None, "tensor"),
            P("dp", None, "tensor"),
            P("tensor", None),
        ),
        out_specs=(P(("dp", "tensor"), None), P("dp", None, "tensor"), P("tensor", None)),
        check_vma=False,
    )
```

profile of v0, /device:TPU:1, one launch (start us, length us, event | category | flops | bytes accessed | tf_op | source)
XLA Modules:
  0.0 620.2 jit_solution(10093013230282823919)
XLA Ops:
  7.2 0.0 all-gather.2.cloned.1.call-start
  7.2 0.7 all-gather.2.cloned.1.call-update
  7.9 0.0 all-reduce.3.cloned.1.call-start
  8.0 0.2 copy-done
  8.2 6.7 %convolution_convert_fusion = bf16[512,5120]{1,0:T(8,128)(2,1)} fusion(bf16[512,384]{1,0:T(8,128)(2,1)S(1)} %copy-done, bf16[5120,384]{1,0:T(8,128)(2,1)} %param.7), kind=kOutput, calls=%fused_computation.2 | convolution fusion | flops 2015887360 | bytes 9568256 | tf_op jit(solution)/shard_map/dot_general | solution.py:17
  14.9 0.0 all-reduce.5.cloned.1.call-start
  15.0 63.3 %all-gather.2.cloned.1.call-done = bf16[512,5120]{1,0:T(8,128)(2,1)} async-done(((bf16[64,5120]{1,0:T(8,128)(2,1)}), bf16[512,5120]{1,0:T(8,128)(2,1)}) %all-gather.2.cloned.1.call-update) | async-done | bytes 5242896 | tf_op jit(solution)/shard_map/all_gather | solution.py:27
  78.3 6.6 %convert_add_fusion = f32[5120,384]{1,0:T(8,128)S(1)} fusion(bf16[512,5120]{1,0:T(8,128)(2,1)} %all-gather.2.cloned.1.call-done, bf16[512,384]{1,0:T(8,128)(2,1)S(1)} %copy-done, bf16[1,5120,384]{2,1,0:T(8,128)(2,1)} %param.8), kind=kOutput, calls=%fused_computation | convolution fusion | flops 2017198080 | bytes 17432576 | tf_op jit(solution)/shard_map/dot_general | solution.py:26
  84.9 3.1 copy-done.1
  88.0 8.3 %fusion.5 = f32[5120,32]{0,1:T(8,128)} fusion(f32[5120,384]{1,0:T(8,128)S(1)} %convert_add_fusion, f32[384,32]{0,1:T(8,128)S(1)} %copy-done.3), kind=kOutput, calls=%fused_computation.17 | convolution fusion | flops 754974720 | bytes 8568832 | tf_op jit(solution)/shard_map/dot_general | solution.py:33
  96.3 0.0 all-reduce.5.cloned.1.call-update
  96.4 111.7 %all-reduce.3.cloned.1.call-done = bf16[512,5120]{1,0:T(8,128)(2,1)} async-done(((bf16[512,5120]{1,0:T(8,128)(2,1)}), bf16[512,5120]{1,0:T(8,128)(2,1)}) %all-reduce.3.cloned.1.call-update) | async-done | bytes 5242896 | tf_op jit(solution)/shard_map/psum | solution.py:16
  208.1 2.0 convert_convert_fusion
  210.0 254.4 %all-reduce.5.cloned.1.call-done = f32[5120,32]{0,1:T(8,128)} async-done(((f32[5120,32]{0,1:T(8,128)}), f32[5120,32]{0,1:T(8,128)}) %all-reduce.5.cloned.1.call-update) | async-done | bytes 655376 | tf_op jit(solution)/shard_map/psum | solution.py:34
  464.4 1.9 fusion.6
  466.4 0.1 copy.8
  466.4 2.9 cholesky.16
  469.4 0.6 compare_reduce_fusion
  470.0 0.7 fusion.1
  470.7 2.4 custom-call.7
  473.1 1.8 fusion.2
  475.0 6.8 %convolution_convert_fusion.1 = bf16[384,32]{0,1:T(8,128)(2,1)S(1)} fusion(f32[5120,384]{1,0:T(8,128)} %copy-done.1, f32[32,5120]{1,0:T(8,128)S(1)} %fusion.2), kind=kOutput, calls=%fused_computation.5 | convolution fusion | flops 754987008 | bytes 8544256 | tf_op jit(solution)/shard_map/dot_general | solution.py:37
  481.8 121.9 %psum.23 = bf16[384,32]{0,1:T(8,128)(2,1)S(1)} all-reduce(bf16[384,32]{0,1:T(8,128)(2,1)S(1)} %convolution_convert_fusion.1), channel_id=1, replica_groups=mesh['dp'=32,'tensor'=8] {'dp'}, use_global_device_ids=true, to_apply=%region_4.5 | all-reduce | flops 12288 | bytes 49152 | tf_op jit(solution)/shard_map/psum | solution.py:40
  603.7 9.9 %fusion = bf16[1,5120,384]{2,1,0:T(8,128)(2,1)} fusion(f32[5120,384]{1,0:T(8,128)} %copy-done.1, f32[32,5120]{1,0:T(8,128)S(1)} %fusion.2, f32[384,32]{0,1:T(8,128)S(1)} %convert_multiply_fusion), kind=kOutput, calls=%fused_computation.3 | convolution fusion | flops 758906880 | bytes 12500992 | tf_op jit(solution)/shard_map/dot_general | solution.py:41
  (10 shorter events, 0.1 us)
Async XLA Ops:
  7.2 1.0 copy-start
  7.2 71.1 %all-gather.2.cloned.1.call-start = ((), (), s32[]{:S(2)}) async-start(), calls=%async_computation.1 | async-start | bytes 5898240 | tf_op jit(solution)/shard_map/all_gather | solution.py:27
  7.9 200.1 %all-reduce.3.cloned.1.call-start = ((), (), s32[]{:S(2)}) async-start(), calls=%async_computation | async-start | bytes 10485760 | tf_op jit(solution)/shard_map/psum | solution.py:16
  14.9 449.5 %all-reduce.5.cloned.1.call-start = ((), (), s32[]{:S(2)}) async-start(), calls=%async_computation.2 | async-start | bytes 1310720 | tf_op jit(solution)/shard_map/psum | solution.py:34
  15.0 73.0 %copy-start.3 = (f32[384,32]{0,1:T(8,128)S(1)}, f32[384,32]{0,1:T(8,128)}, u32[]{:S(2)}) copy-start(f32[384,32]{0,1:T(8,128)} %param.9) | copy-start | bytes 147460
  84.9 3.1 copy-start.1
  603.7 9.9 %copy-start.2 = (f32[384,32]{0,1:T(8,128)}, f32[384,32]{0,1:T(8,128)S(1)}, u32[]{:S(2)}) copy-start(f32[384,32]{0,1:T(8,128)S(1)} %convert_multiply_fusion) | copy-start | bytes 147460
Sparse Core Ops, SparseCore 0:
  9.8 68.4 all-gather.1
  80.7 127.3 all-reduce.2
  214.1 250.2 all-reduce.4
where the time goes:
time: 624 us; the launch traced here: 620 us
  waiting for transfers between devices  430 us (69%)
  blocking collectives  122 us (20%)
  matrix products  42.1 us (7%)
  between operations  13.8 us (2%)
  other arithmetic  8.66 us (1%)
    psum x1, waiting for transfers between devices, local(): p_sum = lax.psum(p_terms, ('dp', 'tensor'))  254 us
    psum x1, blocking collectives, local(): lax.psum(local_q.astype(jnp.bfloat16), 'dp').astype(jnp.float32)  122 us
    psum x1, waiting for transfers between devices, local(): lax.psum(lax.dot_general(rows, weight, (((1,), (1,)), ((), ())), preferre...  112 us
    all_gather x1, waiting for transfers between devices, local(): lax.all_gather(tokens, 'tensor', axis=0, tiled=True)  63.3 us
  transfers between devices with their start and end apart: 3, of which 3 were waited for; matrix products, arithmetic and copies ran while one was open for 4% of the time, Pallas kernels for 0%

commit v1 on v0

v1 whole, which is shorter than its diff:
```python
import functools

import jax
import jax.numpy as jnp
from jax import lax
from jax.experimental import pallas as pl
from jax.experimental.pallas import tpu as pltpu
from jax.sharding import PartitionSpec as P

MESH = pl.DeviceIdType.MESH
F32 = jnp.float32
BF16 = jnp.bfloat16
NY, NX, NZ = 4, 4, 8
NP = NY * NX
R = 32
NN = (((1,), (0,)), ((), ()))
NT = (((1,), (1,)), ((), ()))
TN = (((0,), (0,)), ((), ()))


def mm(a, b, dims):
    return lax.dot_general(a, b, dims, preferred_element_type=F32)


def split3(v):
    hi = v.astype(BF16)
    rest = v - hi.astype(F32)
    mid = rest.astype(BF16)
    low = (rest - mid.astype(F32)).astype(BF16)
    return hi, mid, low


def stack3(v):
    return jnp.concatenate(split3(v), axis=0)


def fold3(v):
    return v[0:R] + v[R : 2 * R] + v[2 * R : 3 * R]


def inverse_factor(gram):
    rows = lax.broadcasted_iota(jnp.int32, (R, 1), 0)
    eye = (
        lax.broadcasted_iota(jnp.int32, (R, R), 0)
        == lax.broadcasted_iota(jnp.int32, (R, R), 1)
    ).astype(F32)
    a = jnp.concatenate([gram, eye], axis=1)
    for j in range(R):
        row = a[j : j + 1, :]
        pivot = a[j : j + 1, j : j + 1]
        factor = jnp.where(rows > j, a[:, j : j + 1] / pivot, 0.0)
        a = a - factor * row
    diag = jnp.sum(a[:, :R] * eye, axis=1, keepdims=True)
    return a[:, R:] / jnp.sqrt(diag)


def main_kernel(
    x_ref, g_ref, q_ref, w_hbm, f_hbm,
    ig_ref, ps_out, qs_out, qn_out,
    f_ref, hb, hr, pb, pcr, ph, ppr, zb, pzr, pfin, ps, yb, yr, qb, qcr, qp, qfin, ga, wa, ob,
    lsem, hs, hrs, cs, crs, rss, rsr, zs, zr, ags, agr, ys, yrs, qps, qpr_s,
    gas, gar, gxs, gxr, gss, gsr, wzs, wzr, wys, wyr, oxs, oxr,
):
    dp = lax.axis_index("dp")
    z = lax.axis_index("tensor")
    plane = dp // 2
    core = lax.rem(dp, 2)
    y, x = plane // NX, lax.rem(plane, NX)
    sign = 1 - 2 * core
    seat = 2 * x + core

    def at(yy, xx, cc, zz):
        return ((yy * NX + xx) * 2 + cc, zz)

    def z_of(k):
        return lax.rem(z + k + 2 * NZ, NZ)

    def x_of(k):
        return lax.rem(x + k + 2 * NX, NX)

    def y_of(k):
        return lax.rem(y + k + 2 * NY, NY)

    def p_of(k):
        return lax.rem(plane + k, NP)

    def rcopy(src, dst, s_sem, r_sem, device):
        return pltpu.make_async_remote_copy(
            src_ref=src, dst_ref=dst, send_sem=s_sem, recv_sem=r_sem,
            device_id=device, device_id_type=MESH,
        )

    sent = []

    def go(copy):
        copy.start()
        sent.append(copy)
        return copy

    sibling = (2 * plane + 1 - core, z)

    f_copies = []
    for i in range(2):
        part = pl.ds(2560 * i, 2560)
        f_copies.append(pltpu.make_async_copy(f_hbm.at[part], f_ref.at[part], lsem.at[i]))
        f_copies[-1].start()

    barrier = pltpu.get_barrier_semaphore()
    peers = [(dp, z_of(k)) for k in range(1, NZ)]
    peers += [(2 * p_of(k) + core, z) for k in range(1, NP)]
    peers += [at(y, x_of(k), 1 - core, z) for k in range(NX)]
    for peer in peers:
        pl.semaphore_signal(barrier, 1, device_id=peer, device_id_type=MESH)

    qs = stack3(q_ref[...].T)
    hfull = fold3(mm(qs, g_ref[...], NT))
    for t in range(4):
        hb[t] = hfull[:, 128 * t : 128 * t + 128]
    pl.semaphore_wait(barrier, len(peers))

    h_copies = []
    for k in range(1, NZ):
        zd = z_of(k)
        h_copies.append(go(rcopy(hb.at[zd // 2], hr.at[k], hs.at[k], hrs.at[k], (dp, zd))))

    def g_rows(s):
        return pl.ds(pl.multiple_of(64 * s, 64), 64)

    def lanes(zz):
        return pl.ds(pl.multiple_of(384 * zz, 128), 384)

    ga_copies = []
    for k in range(1, NZ):
        zd = z_of(k)
        ga_copies.append(
            go(rcopy(g_ref.at[g_rows(zd), :], ga.at[g_rows(seat), lanes(z)], gas.at[k], gar.at[k], (dp, zd)))
        )
    ga[g_rows(seat), lanes(z)] = g_ref[g_rows(z), :]

    def w_rows(yy):
        return pl.ds(pl.multiple_of(160 * yy, 32), 160)

    own_w = w_hbm.at[pl.ds(pl.multiple_of(640 * seat + 160 * y, 32), 160), :]
    own_slot = wa.at[w_rows(y), lanes(z)]
    w_local = pltpu.make_async_copy(own_w, own_slot, lsem.at[2])
    w_local.start()
    ring = [None] * 8

    def w_ring(step, toward, index):
        zz = z_of(-toward * step)
        slot = wa.at[w_rows(y), lanes(zz)]
        src = own_w if step == 0 else slot
        ring[index] = go(rcopy(src, slot, wzs.at[index], wzr.at[index], (dp, z_of(toward))))

    ydev = [at(y_of(sign), x, core, z), at(y_of(-sign), x, core, z)]
    ysent = {}

    def w_share(m, zz):
        slot = wa.at[w_rows(y), lanes(zz)]
        src = own_w if m == 0 else slot
        for i in range(2):
            ysent[m, i] = go(rcopy(src, slot, wys.at[m, i], wyr.at[m, i], ydev[i]))

    def w_relay(m, zz):
        ysent[m, 0].wait_recv()
        slot = wa.at[w_rows(y_of(-sign)), lanes(zz)]
        ysent[m, 2] = go(rcopy(slot, slot, wys.at[m, 2], wyr.at[m, 2], ydev[0]))

    z_from = [z] + [z_of(d * k * sign) for k in range(1, 4) for d in (-1, 1)] + [z_of(4)]

    def w_arrive(m):
        ring[m].wait_recv()
        k = (m + 1) // 2
        if m % 2 == 1 and k < 4:
            w_ring(k, sign, m + 2)
        if m % 2 == 0 and k < 3:
            w_ring(k, -sign, m + 2)
        w_share(m, z_from[m])

    w_ring(0, sign, 1)
    w_ring(0, -sign, 2)
    w_share(0, z)

    for c in f_copies:
        c.wait()

    def f_rows(cb):
        return pl.ds(pl.multiple_of(640 * cb, 640), 640)

    def x_lanes(cb):
        return pl.ds(pl.multiple_of(640 * cb, 128), 640)

    @pl.loop(0, 8)
    def _(cb):
        v = fold3(mm(qs, f_ref[f_rows(cb), :], NT))
        for a in range(4):
            pb[a, cb] = v[8 * a : 8 * a + 8]

    for c in h_copies:
        c.wait_recv()
    hsum = hb[z // 2]
    for k in range(1, NZ):
        hsum = hsum + hr[k]
    hsum = jnp.where(lax.rem(z, 2) == 1, pltpu.roll(hsum, 64, 1), hsum)
    hparts = stack3(hsum[:, :64])

    @pl.loop(0, 8)
    def _(cb):
        v = fold3(mm(hparts, x_ref[:, x_lanes(cb)], NN))
        for a in range(4):
            pb[a, cb] = pb[a, cb] + v[8 * a : 8 * a + 8]

    c_copy = go(rcopy(pb.at[pl.ds(2 * (1 - core), 2)], pcr, cs.at[0], crs.at[0], sibling))
    for c in ga_copies:
        c.wait_recv()
    block = ga.at[g_rows(seat), :]
    xdev = [at(y, x_of(sign), core, z), at(y, x_of(-sign), core, z)]
    gx = [go(rcopy(block, block, gxs.at[i], gxr.at[i], xdev[i])) for i in range(2)]
    gsib = [go(rcopy(block, block, gss.at[0], gsr.at[0], sibling))]
    c_copy.wait_recv()

    @pl.loop(0, 8)
    def _(cb):
        for hh in range(2):
            ph[8 * hh + cb] = pb[2 * core + hh, cb] + pcr[hh, cb]

    rs_copies = []
    for k in range(1, NP):
        pd = p_of(k)
        rs_copies.append(go(rcopy(ph.at[pd], ppr.at[k], rss.at[k], rsr.at[k], (2 * pd + core, z))))
    w_local.wait()
    w_arrive(1)
    w_arrive(2)
    for c in rs_copies:
        c.wait_recv()
    total = ph[plane]
    for k in range(1, NP):
        total = total + ppr[k]
    zb[...] = total
    z_copies = []
    for k in range(1, NZ):
        z_copies.append(go(rcopy(zb, pzr.at[k], zs.at[k], zr.at[k], (dp, z_of(k)))))
    w_arrive(3)
    w_arrive(4)
    for c in z_copies:
        c.wait_recv()
    for k in range(1, NZ):
        total = total + pzr[k]
    own_piece = pfin.at[core, plane]
    own_piece[...] = total
    ag_copies = []
    for k in range(1, NP):
        ag_copies.append(
            go(rcopy(own_piece, own_piece, ags.at[k], agr.at[k], (2 * p_of(k) + core, z)))
        )

    def g_block(xx):
        return ga.at[g_rows(2 * xx + core), :]

    def g_pass(i):
        gx[i].wait_recv()
        blk = g_block(x_of(-sign if i == 0 else (sign if i == 1 else 2)))
        if i == 0:
            gx.append(go(rcopy(blk, blk, gxs.at[2], gxr.at[2], xdev[0])))
        gsib.append(go(rcopy(blk, blk, gss.at[i + 1], gsr.at[i + 1], sibling)))

    g_pass(0)
    g_pass(1)
    for c in ag_copies:
        c.wait_recv()
    half = pfin.at[core]
    cg_copy = go(rcopy(half, half, cs.at[1], crs.at[1], sibling))
    w_arrive(5)
    w_arrive(6)
    cg_copy.wait_recv()

    def p_block(cb):
        return jnp.concatenate([pfin[a // 2, 8 * (a % 2) + cb] for a in range(4)], axis=0)

    def accumulate(cb, carry):
        gram, yt = carry
        parts = stack3(p_block(cb))
        ps[cb] = parts
        gram = gram + mm(parts, parts, NT)
        yt = yt + mm(parts, x_ref[:, x_lanes(cb)], NT)
        return gram, yt

    gram, yt = lax.fori_loop(
        0, 8, accumulate, (jnp.zeros((96, 96), F32), jnp.zeros((96, 64), F32))
    )
    yt = fold3(yt)
    yb[...] = jnp.concatenate([yt, jnp.zeros((R, 64), F32)], axis=1)
    y_copies = []
    for k in range(1, NZ):
        y_copies.append(go(rcopy(yb, yr.at[k], ys.at[k], yrs.at[k], (dp, z_of(k)))))

    qt = lax.fori_loop(
        0, 8, lambda cb, t: t + mm(ps[cb], f_ref[f_rows(cb), :], NN), jnp.zeros((96, 384), F32)
    )
    gram = fold3(gram)
    gram = gram[:, 0:R] + gram[:, R : 2 * R] + gram[:, 2 * R : 3 * R]
    linv = inverse_factor(gram)
    w_arrive(7)
    g_pass(2)

    qt = qt + mm(stack3(yt), g_ref[g_rows(z), :], NN)
    for k in range(1, NZ):
        y_copies[k - 1].wait_recv()
        qt = qt + mm(stack3(yr[k][:, :64]), g_ref[g_rows(z_of(-k)), :], NN)
    qt = fold3(qt)
    for cc in range(2):
        qb[cc] = qt[16 * cc : 16 * cc + 16]
    qc_copy = go(rcopy(qb.at[1 - core], qcr, cs.at[2], crs.at[2], sibling))
    l3 = split3(linv)
    lparts = jnp.concatenate([jnp.concatenate([part] * 3, axis=1) for part in l3], axis=0)
    qc_copy.wait_recv()
    own_q = qp.at[plane]
    own_q[...] = qb[core] + qcr[...]
    q_copies = []
    for k in range(1, NP):
        q_copies.append(go(rcopy(own_q, own_q, qps.at[k], qpr_s.at[k], (2 * p_of(k) + core, z))))

    @pl.loop(0, 8)
    def _(cb):
        hi, mid, low = split3(fold3(mm(lparts, ps[cb], NN)))
        ps_out[cb] = jnp.concatenate([hi, hi, hi, mid, mid, low], axis=0)

    for m in range(4):
        w_relay(m, z_from[m])
    for c in q_copies:
        c.wait_recv()
    qsum = qp[0]
    for p in range(1, NP):
        qsum = qsum + qp[p]
    own_half = qfin.at[core]
    own_half[...] = qsum
    qg_copy = go(rcopy(own_half, own_half, cs.at[3], crs.at[3], sibling))
    for m in range(4, 8):
        w_relay(m, z_from[m])
    qg_copy.wait_recv()
    qall = stack3(jnp.concatenate([qfin[0], qfin[1]], axis=0))
    qn = fold3(mm(lparts, qall, NN)) * (1.0 / 32.0)
    qn_out[...] = qn.T
    hi, mid, low = split3(-qn)
    qs_out[...] = jnp.concatenate([hi, mid, low, hi, mid, hi], axis=0)

    for c in gsib:
        c.wait_recv()
    for m in range(8):
        ysent[m, 1].wait_recv()
        ysent[m, 2].wait_recv()

    def ig_rows(i):
        return pl.ds(pl.multiple_of(128 * i, 128), 128)

    @pl.loop(0, 4)
    def _(i):
        ob[ig_rows(i), :] = mm(ga[ig_rows(i), :], wa[...], NT).astype(BF16)

    own_cols = pl.ds(pl.multiple_of(640 * seat, 128), 640)
    out = []
    for dx in range(NX):
        for other in range(2):
            if dx == 0 and other == 0:
                continue
            i = 2 * dx + other
            xd = x_of(dx)
            cd = core if other == 0 else 1 - core
            out.append(
                go(rcopy(ob.at[g_rows(2 * xd + cd), :], ig_ref.at[:, own_cols], oxs.at[i], oxr.at[i], at(y, xd, cd, z)))
            )
    ig_ref[:, own_cols] = ob[g_rows(seat), :]
    for c in out:
        c.wait_recv()
    for c in sent:
        c.wait_send()


def final_kernel(x_ref, p_ref, g_ref, q_ref, f_ref, o_ref):
    value = mm(x_ref[...], g_ref[...], TN) + mm(p_ref[0], q_ref[...], TN)
    o_ref[...] = (value + f_ref[...].astype(F32)).astype(BF16)


def local(tokens, token_grads, weight, feedback, q_start):
    vmem = pl.BlockSpec(memory_space=pltpu.VMEM)
    hbm = pl.BlockSpec(memory_space=pl.ANY)
    dma = pltpu.SemaphoreType.DMA
    carried = feedback[0]
    every = lax.all_gather(tokens, "tensor", axis=0, tiled=True)
    input_grads, p_parts, q_parts, q_next = pl.pallas_call(
        main_kernel,
        name="factors_and_input_grads",
        out_shape=(
            jax.ShapeDtypeStruct((64, 5120), BF16),
            jax.ShapeDtypeStruct((8, 192, 640), BF16),
            jax.ShapeDtypeStruct((192, 384), BF16),
            jax.ShapeDtypeStruct((384, R), F32),
        ),
        in_specs=[vmem, vmem, vmem, hbm, hbm],
        out_specs=(vmem, vmem, vmem, vmem),
        scratch_shapes=[
            pltpu.VMEM((5120, 384), BF16),
            pltpu.VMEM((4, R, 128), F32),
            pltpu.VMEM((NZ, R, 128), F32),
            pltpu.VMEM((4, 8, 8, 640), F32),
            pltpu.VMEM((2, 8, 8, 640), F32),
            pltpu.VMEM((NP, 8, 640), F32),
            pltpu.VMEM((NP, 8, 640), F32),
            pltpu.VMEM((8, 640), F32),
            pltpu.VMEM((NZ, 8, 640), F32),
            pltpu.VMEM((2, NP, 8, 640), F32),
            pltpu.VMEM((8, 96, 640), BF16),
            pltpu.VMEM((R, 128), F32),
            pltpu.VMEM((NZ, R, 128), F32),
            pltpu.VMEM((2, 16, 384), F32),
            pltpu.VMEM((16, 384), F32),
            pltpu.VMEM((NP, 16, 384), F32),
            pltpu.VMEM((2, 16, 384), F32),
            pltpu.VMEM((512, 3072), BF16),
            pltpu.VMEM((640, 3072), BF16),
            pltpu.VMEM((512, 640), BF16),
            dma((3,)),
            dma((NZ,)), dma((NZ,)),
            dma((4,)), dma((4,)),
            dma((NP,)), dma((NP,)),
            dma((NZ,)), dma((NZ,)),
            dma((NP,)), dma((NP,)),
            dma((NZ,)), dma((NZ,)),
            dma((NP,)), dma((NP,)),
            dma((NZ,)), dma((NZ,)),
            dma((3,)), dma((3,)),
            dma((4,)), dma((4,)),
            dma((8,)), dma((8,)),
            dma((8, 3)), dma((8, 3)),
            dma((8,)), dma((8,)),
        ],
        compiler_params=pltpu.CompilerParams(
            collective_id=0, has_side_effects=True, vmem_limit_bytes=48 * 2**20
        ),
        cost_estimate=pl.CostEstimate(flops=3 * 10**9, bytes_accessed=200 * 10**6, transcendentals=0),
    )(tokens, token_grads, q_start, weight, carried)
    new_feedback = pl.pallas_call(
        final_kernel,
        name="new_feedback",
        grid=(8,),
        out_shape=jax.ShapeDtypeStruct((5120, 384), BF16),
        in_specs=[
            pl.BlockSpec((512, 640), lambda i: (0, i)),
            pl.BlockSpec((1, 192, 640), lambda i: (i, 0, 0)),
            pl.BlockSpec((512, 384), lambda i: (0, 0)),
            pl.BlockSpec((192, 384), lambda i: (0, 0)),
            pl.BlockSpec((640, 384), lambda i: (i, 0)),
        ],
        out_specs=pl.BlockSpec((640, 384), lambda i: (i, 0)),
        compiler_params=pltpu.CompilerParams(vmem_limit_bytes=32 * 2**20),
        cost_estimate=pl.CostEstimate(
            flops=2 * 704 * 5120 * 384, bytes_accessed=15 * 10**6, transcendentals=0
        ),
    )(every, p_parts, token_grads, q_parts, carried)
    return input_grads, new_feedback[None], q_next


def solution(mesh):
    return jax.shard_map(
        local,
        mesh=mesh,
        in_specs=(
            P(("dp", "tensor"), None),
            P("dp", "tensor"),
            P(None, "tensor"),
            P("dp", None, "tensor"),
            P("tensor", None),
        ),
        out_specs=(P(("dp", "tensor"), None), P("dp", None, "tensor"), P("tensor", None)),
        check_vma=False,
    )
```

time: 624 us -> 134 us (0.21)
  waiting for transfers between devices: 430 us -> 0.68 us
  blocking collectives: 122 us -> 0 us
  Pallas kernels: 0 us -> 110 us
  matrix products: 42.1 us -> 0 us
  other arithmetic: 8.66 us -> 0 us
    psum x2 -> x0, waiting for transfers between devices: 366 us -> none  [the longest x1 254 us: local(): p_sum = lax.psum(p_terms, ('dp', 'tensor'))]
    psum x1 -> x0, blocking collectives: 122 us -> none  [local(): lax.psum(local_q.astype(jnp.bfloat16), 'dp').astype(jnp.float32)]
    pallas_call x0 -> x2, Pallas kernels: none -> 110 us  [the longest x1 103 us: local(): pl.pallas_call(main_kernel, name='factors_and_input_grads', out_shape=(ja...]
    all_gather x1, waiting for transfers between devices: 63.3 us -> 0.01 us  [local(): every = lax.all_gather(tokens, 'tensor', axis=0, tiled=True)]
    dot_general x6 -> x0, matrix products: 40.3 us -> none  [the longest x1 9.91 us: local(): decompressed = jnp.dot(p_hat, q_next.T, precision=lax.Precision.HIGHEST)]
    another operation x5 -> x0, other arithmetic: 6.68 us -> none  [the longest x3 3.6 us: local(): p_hat = lower_solve(jnp.linalg.cholesky(gram_matrix), p_sum)]
  transfers between devices with their start and end apart: 3 -> 1, of which waited for: 3 -> 0; matrix products, arithmetic and copies ran while one was open for 4% -> 1% of each run, Pallas kernels for 0% -> 77%
where the time goes in v1:
time: 134 us
  Pallas kernels  110 us (82%)
  between operations  14.1 us (11%)
  local copies, waits for them, and re-layouts  9.17 us (7%)
    pallas_call x1, Pallas kernels, local(): pl.pallas_call(main_kernel, name='factors_and_input_grads', out_shape=(ja...  103 us
    unnamed x13, local copies, waits for them, and re-layouts  9.17 us
    pallas_call x1, Pallas kernels, local(): pl.pallas_call(final_kernel, name='new_feedback', grid=(8,), out_shape=ja...  7.18 us
  transfers between devices with their start and end apart: 1, of which 0 were waited for; matrix products, arithmetic and copies ran while one was open for 1% of the time, Pallas kernels for 77%

profile of v1, /device:TPU:1, one launch (start us, length us, event | category | flops | bytes accessed | tf_op | source)
XLA Modules:
  0.0 133.8 jit_solution(18038882899197611418)
XLA Ops:
  7.2 0.0 all-gather.2.cloned.1.call-start
  7.2 0.7 all-gather.2.cloned.1.call-update
  7.9 0.9 copy.8.q_ref
  8.8 0.0 copy-start.2
  8.8 1.1 copy-done.2
  9.9 0.0 copy-start.3
  9.9 1.0 copy-done.3
  10.9 0.0 copy-start.4
  10.9 102.7 %factors_and_input_grads.1 = (bf16[64,5120]{1,0:T(8,128)(2,1)S(1)}, bf16[8,192,640]{2,1,0:T(8,128)(2,1)S(1)}, bf16[192,384]{1,0:T(8,128)(2,1)S(1)}, f32[384,32]{1,0:T(8,128)S(1)}) custom-call(bf16[64,5120]{1,0:T(8,128)(2,1)S(1)} %copy-done.2, bf16[512,384]{1,0:T(8,128)(2,1)S(1)} %copy-done.3, f32[384,32]{1,0:T(8,128)S(1)} %copy.8.q_ref, ...), custom_call_target="tpu_custom_call" | custom-call | flops 3000000000 | bytes 200000000 | tf_op jit(solution)/shard_map/factors_and_input_grads/pallas_call | solution.py:390
  113.6 0.7 copy.9
  114.3 0.0 all-gather.2.cloned.1.call-done.x_ref
  114.3 0.0 copy-done.4
  114.3 0.0 copy-start
  114.3 2.5 %copy-done = bf16[512,5120]{1,0:T(8,128)(2,1)S(1)} copy-done((bf16[512,5120]{1,0:T(8,128)(2,1)S(1)}, bf16[512,5120]{1,0:T(8,128)(2,1)}, u32[]{:S(2)}) %copy-start) | copy-done | bytes 5242904
  116.8 0.0 copy-start.1
  116.8 2.1 %copy-done.1 = bf16[1,5120,384]{2,1,0:T(8,128)(2,1)S(1)} copy-done((bf16[1,5120,384]{2,1,0:T(8,128)(2,1)S(1)}, bf16[1,5120,384]{2,1,0:T(8,128)(2,1)}, u32[]{:S(2)}) %copy-start.1) | copy-done | bytes 3932184
  118.9 7.2 %new_feedback.1 = bf16[5120,384]{1,0:T(8,128)(2,1)} custom-call(bf16[512,5120]{1,0:T(8,128)(2,1)S(1)} %copy-done, bf16[8,192,640]{2,1,0:T(8,128)(2,1)S(1)} %get-tuple-element.8.p_ref, bf16[512,384]{1,0:T(8,128)(2,1)S(1)} %copy-done.4, bf16[192,384]{1,0:T(8,128)(2,1)S(1)} %get-tuple-element.9.q_ref, bf16[5120,384]{1,0:T(8,128)(2,1)S(1)} %bitcast.3), custom_call_target="tpu_custom_call" | custom-call | flops 2768240640 | bytes 15000000 | tf_op jit(solution)/shard_map/new_feedback/pallas_call | solution.py:442
  126.1 0.8 copy.11
Async XLA Ops:
  7.2 107.2 %all-gather.2.cloned.1.call-start = ((), (), s32[]{:S(2)}) async-start(), calls=%async_computation | async-start | bytes 5898240 | tf_op jit(solution)/shard_map/all_gather | solution.py:389
  8.8 1.1 copy-start.2
  9.9 1.0 copy-start.3
  10.9 103.4 %copy-start.4 = (bf16[512,384]{1,0:T(8,128)(2,1)S(1)}, bf16[512,384]{1,0:T(8,128)(2,1)}, u32[]{:S(2)}) copy-start(bf16[512,384]{1,0:T(8,128)(2,1)} %g_ref.3) | copy-start | bytes 1179652
  114.3 2.5 %copy-start = (bf16[512,5120]{1,0:T(8,128)(2,1)S(1)}, bf16[512,5120]{1,0:T(8,128)(2,1)}, u32[]{:S(2)}) copy-start(bf16[512,5120]{1,0:T(8,128)(2,1)} %all-gather.2.cloned.1.call-done.x_ref) | copy-start | bytes 15728644
  116.8 2.1 %copy-start.1 = (bf16[1,5120,384]{2,1,0:T(8,128)(2,1)S(1)}, bf16[1,5120,384]{2,1,0:T(8,128)(2,1)}, u32[]{:S(2)}) copy-start(bf16[1,5120,384]{2,1,0:T(8,128)(2,1)} %param.8) | copy-start | bytes 11796484
Sparse Core Ops, SparseCore 0:
  9.8 90.6 all-gather.1

commit v2 on v0

v2 whole, which is shorter than its diff:
```python
import jax
import jax.numpy as jnp
from jax import lax
from jax.experimental import pallas as pl
from jax.experimental.pallas import tpu as pltpu
from jax.sharding import PartitionSpec as P

MESH = pl.DeviceIdType.MESH
F32 = jnp.float32
BF16 = jnp.bfloat16
NY, NX, NZ = 4, 4, 8
NP = NY * NX
R = 32
NN = (((1,), (0,)), ((), ()))
NT = (((1,), (1,)), ((), ()))
TN = (((0,), (0,)), ((), ()))


def mm(a, b, dims):
    return lax.dot_general(a, b, dims, preferred_element_type=F32)


def split3(v):
    hi = v.astype(BF16)
    rest = v - hi.astype(F32)
    mid = rest.astype(BF16)
    low = (rest - mid.astype(F32)).astype(BF16)
    return hi, mid, low


def stack3(v):
    return jnp.concatenate(split3(v), axis=0)


def fold3(v):
    return v[0:R] + v[R : 2 * R] + v[2 * R : 3 * R]


def inverse_factor(gram):
    rows = lax.broadcasted_iota(jnp.int32, (R, 1), 0)
    eye = (
        lax.broadcasted_iota(jnp.int32, (R, R), 0)
        == lax.broadcasted_iota(jnp.int32, (R, R), 1)
    ).astype(F32)
    a = jnp.concatenate([gram, eye], axis=1)
    for j in range(R):
        row = a[j : j + 1, :]
        pivot = a[j : j + 1, j : j + 1]
        factor = jnp.where(rows > j, a[:, j : j + 1] / pivot, 0.0)
        a = a - factor * row
    diag = jnp.sum(a[:, :R] * eye, axis=1, keepdims=True)
    return a[:, R:] / jnp.sqrt(diag)


def main_kernel(
    x_hbm, g_hbm, q_hbm, w_hbm, f_hbm,
    ig_ref, nf_ref, qn_ref,
    g_ref, q_ref, f_ref, xa, acc, pst, qst, hb, hr, pb, pcr, ph, ppr, zb, pzr, zf, pfin, ps, yb, yr,
    qb, qcr, qp, qfin, ga, wa, cols, ob,
    lsem, hs, hrs, cs, crs, rss, rsr, zs, zr, zgs, zgr, ags, agr, ys, yrs, qps, qpr_s,
    gas, gar, gxs, gxr, gss, gsr, wzs, wzr, wys, wyr, oxs, oxr, tls, tlr, tss, tsr,
):
    dp = lax.axis_index("dp")
    z = lax.axis_index("tensor")
    plane = dp // 2
    core = lax.rem(dp, 2)
    y, x = plane // NX, lax.rem(plane, NX)
    sign = 1 - 2 * core
    seat = 2 * x + core

    def at(yy, xx, cc, zz):
        return ((yy * NX + xx) * 2 + cc, zz)

    def z_of(k):
        return lax.rem(z + k + 2 * NZ, NZ)

    def x_of(k):
        return lax.rem(x + k + 2 * NX, NX)

    def y_of(k):
        return lax.rem(y + k + 2 * NY, NY)

    def p_of(k):
        return lax.rem(plane + k, NP)

    sent, pending = [], {}

    def go(src, dst, s_sem, r_sem, device):
        copy = pltpu.make_async_remote_copy(
            src_ref=src, dst_ref=dst, send_sem=s_sem, recv_sem=r_sem,
            device_id=device, device_id_type=MESH,
        )
        copy.start()
        sent.append(copy)
        pending[id(copy)] = copy
        return copy

    def got(copy):
        copy.wait_recv()
        del pending[id(copy)]

    sibling = (2 * plane + 1 - core, z)

    def g_rows(s):
        return pl.ds(pl.multiple_of(64 * s, 64), 64)

    def lanes(zz):
        return pl.ds(pl.multiple_of(384 * zz, 128), 384)

    def f_rows(cb):
        return pl.ds(pl.multiple_of(640 * cb, 640), 640)

    def x_lanes(cb):
        return pl.ds(pl.multiple_of(640 * cb, 128), 640)

    z_from = [z] + [z_of(d * k * sign) for k in range(1, 4) for d in (-1, 1)] + [z_of(4)]
    xdev = [at(y, x_of(sign), core, z), at(y, x_of(-sign), core, z)]
    ydev = [at(y_of(sign), x, core, z), at(y_of(-sign), x, core, z)]
    zdev = [(dp, z_of(sign)), (dp, z_of(-sign))]

    tl, ts = {}, {}

    def tick(t):
        k, part = t // 4, pl.ds(1280 * (t % 4), 1280)
        if k > 0:
            got(tl[t - 4])
        out = xa.at[z_of(-sign * k), :, part]
        tl[t] = go(out, out, tls.at[t], tlr.at[t], zdev[0])
        if k > 0 and t - 4 in ts:
            got(ts[t - 4])
        if k < 3:
            out = xa.at[z_of(sign * k), :, part]
            ts[t] = go(out, out, tss.at[t], tsr.at[t], zdev[1])

    def w_rows(yy):
        return pl.ds(pl.multiple_of(160 * yy, 32), 160)

    own_w = w_hbm.at[pl.ds(pl.multiple_of(640 * seat + 160 * y, 32), 160), :]
    ring, wy = {}, {}

    def w_ring(step, i, index):
        zz = z_of((-sign if i == 0 else sign) * step)
        slot = wa.at[w_rows(y), lanes(zz)]
        ring[index] = go(own_w if step == 0 else slot, slot, wzs.at[index], wzr.at[index], zdev[i])

    def w_share(m):
        slot = wa.at[w_rows(y), lanes(z_from[m])]
        for i in range(2):
            wy[m, i] = go(own_w if m == 0 else slot, slot, wys.at[m, i], wyr.at[m, i], ydev[i])

    def w_relay(m):
        got(wy[m, 0])
        slot = wa.at[w_rows(y_of(-sign)), lanes(z_from[m])]
        wy[m, 2] = go(slot, slot, wys.at[m, 2], wyr.at[m, 2], ydev[0])

    def w_forward(m):
        got(ring[m])
        k = (m + 1) // 2
        if m % 2 == 1 and k < 4:
            w_ring(k, 0, m + 2)
        if m % 2 == 0 and k < 3:
            w_ring(k, 1, m + 2)

    gx, gsib = {}, {}

    def g_block(xx):
        return ga.at[g_rows(2 * xx + core), :]

    def g_share():
        for c in st["ga"]:
            got(c)
        blk = g_block(x)
        for i in range(2):
            gx[i] = go(blk, blk, gxs.at[i], gxr.at[i], xdev[i])
        gsib[0] = go(blk, blk, gss.at[0], gsr.at[0], sibling)

    def g_pass(i):
        got(gx[i])
        blk = g_block(x_of((-sign, sign, 2)[i]))
        if i == 0:
            gx[2] = go(blk, blk, gxs.at[2], gxr.at[2], xdev[0])
        gsib[i + 1] = go(blk, blk, gss.at[i + 1], gsr.at[i + 1], sibling)

    def merge(cb, ms, factors=False):
        grads = [g_ref[g_rows(z_from[m]), :] for m in ms]
        rows = [xa[z_from[m], :, x_lanes(cb)] for m in ms]
        if factors:
            grads.append(qst[...])
            rows.append(pst[cb])
        before = f_ref[f_rows(cb), :].astype(F32) if 0 in ms else acc[cb]
        return before + mm(jnp.concatenate(rows, axis=0), jnp.concatenate(grads, axis=0), TN)

    def columns(ms):
        if 0 in ms:
            for i in range(4):
                got(gsib[i])
        for m in ms:
            got(wy[m, 1])
            got(wy[m, 2])

        @pl.loop(0, 2)
        def _(i):
            rows = pl.ds(pl.multiple_of(256 * i, 256), 256)
            v = sum(mm(ga[rows, lanes(z_from[m])], wa[:, lanes(z_from[m])], NT) for m in ms)
            if 0 in ms:
                cols[rows, :] = v
            else:
                ob[rows, :] = (cols[rows, :] + v).astype(BF16)

    st = {}

    def start():
        loads = [
            pltpu.make_async_copy(q_hbm, q_ref, lsem.at[0]),
            pltpu.make_async_copy(g_hbm, g_ref, lsem.at[1]),
            pltpu.make_async_copy(x_hbm, xa.at[z], lsem.at[2]),
            pltpu.make_async_copy(f_hbm, f_ref, lsem.at[3]),
            pltpu.make_async_copy(own_w, wa.at[w_rows(y), lanes(z)], lsem.at[4]),
        ]
        for c in loads:
            c.start()
        barrier = pltpu.get_barrier_semaphore()
        peers = [(dp, z_of(k)) for k in range(1, NZ)]
        peers += [(2 * p_of(k) + core, z) for k in range(1, NP)]
        peers += [at(y, x_of(k), 1 - core, z) for k in range(NX)]
        for peer in peers:
            pl.semaphore_signal(barrier, 1, device_id=peer, device_id_type=MESH)
        loads[0].wait()
        st["qs"] = qs = stack3(q_ref[...])
        loads[1].wait()
        h = fold3(mm(qs, g_ref[...], NT))
        for s in range(NZ):
            v = h[:, 64 * s : 64 * s + 64]
            hb[s] = jnp.concatenate([v[:16], v[16:]], axis=1)
        pl.semaphore_wait(barrier, len(peers))
        st["h"] = []
        for k in range(1, NZ):
            zd = z_of(k)
            st["h"].append(go(hb.at[zd], hr.at[k], hs.at[k], hrs.at[k], (dp, zd)))
        w_ring(0, 0, 1)
        w_ring(0, 1, 2)
        st["ga"] = []
        for k in range(1, NZ):
            zd = z_of(k)
            slot = ga.at[g_rows(seat), lanes(z)]
            st["ga"].append(go(g_ref.at[g_rows(zd), :], slot, gas.at[k], gar.at[k], (dp, zd)))
        w_share(0)
        ga[g_rows(seat), lanes(z)] = g_ref[g_rows(z), :]
        for c in loads[2:]:
            c.wait()
        tick(0)

    def left():
        qs = st["qs"]

        @pl.loop(0, 8)
        def _(cb):
            v = fold3(mm(qs, f_ref[f_rows(cb), :], NT))
            for a in range(4):
                pb[a, cb] = v[8 * a : 8 * a + 8]

        for c in st["h"]:
            got(c)
        hsum = hb[z]
        for k in range(1, NZ):
            hsum = hsum + hr[k]
        hparts = stack3(jnp.concatenate([hsum[:, :64], hsum[:, 64:]], axis=0))

        @pl.loop(0, 8)
        def _(cb):
            v = fold3(mm(hparts, xa[z, :, x_lanes(cb)], NN))
            for a in range(4):
                pb[a, cb] = pb[a, cb] + v[8 * a : 8 * a + 8]

    def sum_cores():
        c = go(pb.at[pl.ds(2 * (1 - core), 2)], pcr, cs.at[0], crs.at[0], sibling)
        w_forward(1)
        w_forward(2)
        got(c)

        @pl.loop(0, 8)
        def _(cb):
            for hh in range(2):
                ph[8 * hh + cb] = pb[2 * core + hh, cb] + pcr[hh, cb]

    def sum_plane():
        copies = []
        for k in range(1, NP):
            pd = p_of(k)
            copies.append(go(ph.at[pd], ppr.at[k], rss.at[k], rsr.at[k], (2 * pd + core, z)))
        g_share()
        w_share(1)
        w_share(2)
        for c in copies:
            got(c)
        total = ph[plane]
        for k in range(1, NP):
            total = total + ppr[k]
        for r in range(NZ):
            zb[r] = total[r : r + 1]

    def sum_ring():
        copies = []
        for k in range(1, NZ):
            zd = z_of(k)
            copies.append(go(zb.at[zd], pzr.at[k], zs.at[k], zr.at[k], (dp, zd)))
        tick(1)
        for c in copies:
            got(c)
        total = zb[z]
        for k in range(1, NZ):
            total = total + pzr[k]
        zf[z] = total
        own = zf.at[z]
        copies = [go(own, own, zgs.at[k], zgr.at[k], (dp, z_of(k))) for k in range(1, NZ)]
        w_forward(3)
        w_forward(4)
        tick(2)
        w_share(3)
        w_share(4)
        w_relay(0)
        for c in copies:
            got(c)
        pfin[core, plane] = jnp.concatenate([zf[r] for r in range(NZ)], axis=0)

    def spread():
        own = pfin.at[core, plane]
        copies = []
        for k in range(1, NP):
            copies.append(go(own, own, ags.at[k], agr.at[k], (2 * p_of(k) + core, z)))
        tick(3)
        w_relay(1)
        g_pass(0)
        g_pass(1)
        w_forward(5)
        w_forward(6)
        for c in copies:
            got(c)
        half = pfin.at[core]
        c = go(half, half, cs.at[1], crs.at[1], sibling)
        w_share(5)
        w_share(6)
        tick(4)
        got(c)

    def right():
        def block(cb, carry):
            gram, yt = carry
            parts = stack3(
                jnp.concatenate([pfin[a // 2, 8 * (a % 2) + cb] for a in range(4)], axis=0)
            )
            ps[cb] = parts
            gram = gram + mm(parts, parts, NT)
            yt = yt + mm(parts, xa[z, :, x_lanes(cb)], NT)
            return gram, yt

        gram, yt = lax.fori_loop(
            0, 8, block, (jnp.zeros((96, 96), F32), jnp.zeros((96, 64), F32))
        )
        yt = fold3(yt)
        gram = fold3(gram)
        st["gram"] = gram[:, 0:R] + gram[:, R : 2 * R] + gram[:, 2 * R : 3 * R]
        yb[...] = jnp.concatenate([yt[:16], yt[16:]], axis=1)
        copies = [go(yb, yr.at[k], ys.at[k], yrs.at[k], (dp, z_of(k))) for k in range(1, NZ)]
        w_forward(7)
        w_share(7)
        tick(5)
        w_relay(2)
        w_relay(3)
        qt = lax.fori_loop(
            0, 8, lambda cb, t: t + mm(ps[cb], f_ref[f_rows(cb), :], NN), jnp.zeros((96, 384), F32)
        )
        qt = qt + mm(stack3(yt), g_ref[g_rows(z), :], NN)
        linv = inverse_factor(st["gram"])
        st["l"] = jnp.concatenate(
            [jnp.concatenate([part] * 3, axis=1) for part in split3(linv)], axis=0
        )
        g_pass(2)
        for c in copies:
            got(c)
        for k in range(1, NZ):
            v = yr[k]
            yk = stack3(jnp.concatenate([v[:, :64], v[:, 64:]], axis=0))
            qt = qt + mm(yk, g_ref[g_rows(z_of(-k)), :], NN)
        qt = fold3(qt)
        for cc in range(2):
            qb[cc] = qt[16 * cc : 16 * cc + 16]

    def sum_right():
        c = go(qb.at[1 - core], qcr, cs.at[2], crs.at[2], sibling)
        tick(6)
        got(c)
        own = qp.at[plane]
        own[...] = qb[core] + qcr[...]
        copies = []
        for k in range(1, NP):
            copies.append(go(own, own, qps.at[k], qpr_s.at[k], (2 * p_of(k) + core, z)))
        tick(7)
        w_relay(4)
        w_relay(5)
        lparts = st["l"]

        @pl.loop(0, 8)
        def _(cb):
            hi, mid, low = split3(fold3(mm(lparts, ps[cb], NN)))
            pst[cb] = jnp.concatenate([hi, hi, hi, mid, mid, low], axis=0)

        tick(8)

        @pl.loop(0, 8)
        def _(cb):
            acc[cb] = merge(cb, [0, 1, 2])

        for c in copies:
            got(c)
        total = qp[0]
        for p in range(1, NP):
            total = total + qp[p]
        own = qfin.at[core]
        own[...] = total
        c = go(own, own, cs.at[3], crs.at[3], sibling)
        w_relay(6)
        w_relay(7)
        tick(9)
        columns([0, 1, 2, 3])
        got(c)
        qall = stack3(jnp.concatenate([qfin[0], qfin[1]], axis=0))
        qn = fold3(mm(lparts, qall, NN)) * (1.0 / 32.0)
        qn_ref[...] = qn
        hi, mid, low = split3(-qn)
        qst[...] = jnp.concatenate([hi, mid, low, hi, mid, hi], axis=0)

    def finish():
        tick(10)
        columns([4, 5, 6, 7])
        own_cols = pl.ds(pl.multiple_of(640 * seat, 128), 640)
        out = []
        for dx in range(NX):
            for other in range(2):
                if dx == 0 and other == 0:
                    continue
                i = 2 * dx + other
                xd = x_of(dx)
                cd = core if other == 0 else 1 - core
                out.append(
                    go(
                        ob.at[g_rows(2 * xd + cd), :], ig_ref.at[:, own_cols],
                        oxs.at[i], oxr.at[i], at(y, xd, cd, z),
                    )
                )
        ig_ref[:, own_cols] = ob[g_rows(seat), :]
        tick(11)

        @pl.loop(0, 8)
        def _(cb):
            acc[cb] = merge(cb, [3, 4], factors=True)

        for t in range(12, 16):
            tick(t)
        for t in range(4):
            got(tl[12 + t])

            @pl.loop(2 * t, 2 * t + 2)
            def _(cb):
                nf_ref[f_rows(cb), :] = merge(cb, [5, 6, 7]).astype(BF16)

        for c in out:
            got(c)

    steps = [
        start, left, sum_cores, sum_plane, sum_ring, spread, right, sum_right, finish,
    ]
    for step in steps:
        step()
    for c in sent:
        c.wait_send()


def store_kernel(a, b, c, a_out, b_out, c_out, sems):
    copies = [
        pltpu.make_async_copy(src, dst, sems.at[i])
        for i, (src, dst) in enumerate(((a, a_out), (b, b_out), (c, c_out)))
    ]
    for copy in copies:
        copy.start()
    for copy in copies:
        copy.wait()


def local(tokens, token_grads, weight, feedback, q_start):
    vmem = pl.BlockSpec(memory_space=pltpu.VMEM)
    hbm = pl.BlockSpec(memory_space=pl.ANY)
    dma = pltpu.SemaphoreType.DMA
    operands = (tokens, token_grads, q_start.T, weight, feedback[0])
    input_grads, new_feedback, q_next = pl.pallas_call(
        main_kernel,
        name="all_steps",
        out_shape=(
            jax.ShapeDtypeStruct((64, 5120), BF16),
            jax.ShapeDtypeStruct((5120, 384), BF16),
            jax.ShapeDtypeStruct((R, 384), F32),
        ),
        in_specs=[pl.BlockSpec(memory_space=pltpu.HBM)] * 5,
        out_specs=(vmem, vmem, vmem),
        scratch_shapes=[
            pltpu.VMEM((512, 384), BF16),
            pltpu.VMEM((R, 384), F32),
            pltpu.VMEM((5120, 384), BF16),
            pltpu.VMEM((NZ, 64, 5120), BF16),
            pltpu.VMEM((8, 640, 384), F32),
            pltpu.VMEM((8, 192, 640), BF16),
            pltpu.VMEM((192, 384), BF16),
            pltpu.VMEM((NZ, 16, 128), F32),
            pltpu.VMEM((NZ, 16, 128), F32),
            pltpu.VMEM((4, 8, 8, 640), F32),
            pltpu.VMEM((2, 8, 8, 640), F32),
            pltpu.VMEM((NP, 8, 640), F32),
            pltpu.VMEM((NP, 8, 640), F32),
            pltpu.VMEM((NZ, 1, 640), F32),
            pltpu.VMEM((NZ, 1, 640), F32),
            pltpu.VMEM((NZ, 1, 640), F32),
            pltpu.VMEM((2, NP, 8, 640), F32),
            pltpu.VMEM((8, 96, 640), BF16),
            pltpu.VMEM((16, 128), F32),
            pltpu.VMEM((NZ, 16, 128), F32),
            pltpu.VMEM((2, 16, 384), F32),
            pltpu.VMEM((16, 384), F32),
            pltpu.VMEM((NP, 16, 384), F32),
            pltpu.VMEM((2, 16, 384), F32),
            pltpu.VMEM((512, 3072), BF16),
            pltpu.VMEM((640, 3072), BF16),
            pltpu.VMEM((512, 640), F32),
            pltpu.VMEM((512, 640), BF16),
            dma((5,)),
            dma((NZ,)), dma((NZ,)),
            dma((4,)), dma((4,)),
            dma((NP,)), dma((NP,)),
            dma((NZ,)), dma((NZ,)),
            dma((NZ,)), dma((NZ,)),
            dma((NP,)), dma((NP,)),
            dma((NZ,)), dma((NZ,)),
            dma((NP,)), dma((NP,)),
            dma((NZ,)), dma((NZ,)),
            dma((3,)), dma((3,)),
            dma((4,)), dma((4,)),
            dma((8,)), dma((8,)),
            dma((8, 3)), dma((8, 3)),
            dma((8,)), dma((8,)),
            dma((16,)), dma((16,)),
            dma((12,)), dma((12,)),
        ],
        compiler_params=pltpu.CompilerParams(
            collective_id=0, has_side_effects=True, vmem_limit_bytes=42 * 2**20
        ),
        cost_estimate=pl.CostEstimate(flops=5 * 10**9, bytes_accessed=13 * 10**6, transcendentals=0),
    )(*(pltpu.with_memory_space_constraint(a, pltpu.HBM) for a in operands))
    results = (input_grads, new_feedback, q_next)
    input_grads, new_feedback, q_next = pl.pallas_call(
        store_kernel,
        name="store",
        out_shape=tuple(jax.ShapeDtypeStruct(r.shape, r.dtype) for r in results),
        in_specs=[vmem] * 3,
        out_specs=(hbm,) * 3,
        scratch_shapes=[dma((3,))],
        compiler_params=pltpu.CompilerParams(vmem_limit_bytes=2**20),
    )(*results)
    return input_grads, new_feedback[None], q_next.T


def solution(mesh):
    return jax.shard_map(
        local,
        mesh=mesh,
        in_specs=(
            P(("dp", "tensor"), None),
            P("dp", "tensor"),
            P(None, "tensor"),
            P("dp", None, "tensor"),
            P("tensor", None),
        ),
        out_specs=(P(("dp", "tensor"), None), P("dp", None, "tensor"), P("tensor", None)),
        check_vma=False,
    )
```

time: 624 us -> 90.6 us (0.15)
  waiting for transfers between devices: 430 us -> 0 us
  blocking collectives: 122 us -> 0 us
  Pallas kernels: 0 us -> 89.9 us
  matrix products: 42.1 us -> 0 us
  between operations: 13.8 us -> 0.64 us
  other arithmetic: 8.66 us -> 0 us
    psum x2 -> x0, waiting for transfers between devices: 366 us -> none  [the longest x1 254 us: local(): p_sum = lax.psum(p_terms, ('dp', 'tensor'))]
    psum x1 -> x0, blocking collectives: 122 us -> none  [local(): lax.psum(local_q.astype(jnp.bfloat16), 'dp').astype(jnp.float32)]
    pallas_call x0 -> x2, Pallas kernels: none -> 89.9 us  [the longest x1 87.7 us: local(): pl.pallas_call(main_kernel, name='all_steps', out_shape=(jax.ShapeDtypeSt...]
    all_gather x1 -> x0, waiting for transfers between devices: 63.3 us -> none  [local(): lax.all_gather(tokens, 'tensor', axis=0, tiled=True)]
    dot_general x6 -> x0, matrix products: 40.3 us -> none  [the longest x1 9.91 us: local(): decompressed = jnp.dot(p_hat, q_next.T, precision=lax.Precision.HIGHEST)]
    another operation x5 -> x0, other arithmetic: 6.68 us -> none  [the longest x3 3.6 us: local(): p_hat = lower_solve(jnp.linalg.cholesky(gram_matrix), p_sum)]
  transfers between devices with their start and end apart: 3 -> 0, of which waited for: 3 -> 0; matrix products, arithmetic and copies ran while one was open for 4% -> 0% of each run, Pallas kernels for 0% -> 0%
where the time goes in v2:
time: 90.6 us; the launch traced here: 90.5 us
  Pallas kernels  89.9 us (99%)
    pallas_call x1, Pallas kernels, local(): pl.pallas_call(main_kernel, name='all_steps', out_shape=(jax.ShapeDtypeSt...  87.7 us
    pallas_call x1, Pallas kernels, local(): pl.pallas_call(store_kernel, name='store', out_shape=tuple((jax.ShapeDtyp...  2.17 us

profile of v2, /device:TPU:1, one launch (start us, length us, event | category | flops | bytes accessed | tf_op | source)
XLA Modules:
  0.0 90.5 jit_solution(13004700408885601435)
XLA Ops:
  0.6 87.7 %all_steps.1 = (bf16[64,5120]{1,0:T(8,128)(2,1)S(1)}, bf16[5120,384]{1,0:T(8,128)(2,1)S(1)}, f32[32,384]{1,0:T(8,128)S(1)}) custom-call(bf16[64,5120]{1,0:T(8,128)(2,1)} %x_hbm.1, bf16[512,384]{1,0:T(8,128)(2,1)} %g_hbm.1, f32[32,384]{1,0:T(8,128)} %bitcast.6, bf16[5120,384]{1,0:T(8,128)(2,1)} %w_hbm.1, bf16[5120,384]{1,0:T(8,128)(2,1)} %bitcast.4), custom_call_target="tpu_custom_call" | custom-call | flops 5000000000 | bytes 13000000 | tf_op jit(solution)/shard_map/all_steps/pallas_call | solution.py:495
  88.4 2.2 %store.1 = (bf16[64,5120]{1,0:T(8,128)(2,1)}, bf16[5120,384]{1,0:T(8,128)(2,1)}, f32[32,384]{1,0:T(8,128)}) custom-call(bf16[64,5120]{1,0:T(8,128)(2,1)S(1)} %get-tuple-element.9.a, bf16[5120,384]{1,0:T(8,128)(2,1)S(1)} %get-tuple-element.10.b, f32[32,384]{1,0:T(8,128)S(1)} %get-tuple-element.11.c), custom_call_target="tpu_custom_call" | custom-call | tf_op jit(solution)/shard_map/store/pallas_call | solution.py:558

commit v3 on v2

--- a/solution.py
+++ b/solution.py
@@ -83,7 +83,7 @@
     def p_of(k):
         return lax.rem(plane + k, NP)
 
-    sent, pending = [], {}
+    sent, pending, settled = [], {}, [0, 0]
 
     def go(src, dst, s_sem, r_sem, device):
         copy = pltpu.make_async_remote_copy(
@@ -94,6 +94,12 @@
         sent.append(copy)
         pending[id(copy)] = copy
         return copy
+
+    def settle():
+        while settled[0] < settled[1]:
+            sent[settled[0]].wait_send()
+            settled[0] += 1
+        settled[1] = len(sent)
 
     def got(copy):
         copy.wait_recv()
@@ -206,6 +212,24 @@
                 cols[rows, :] = v
             else:
                 ob[rows, :] = (cols[rows, :] + v).astype(BF16)
+
+    def send_columns():
+        own_cols = pl.ds(pl.multiple_of(640 * seat, 128), 640)
+        st["out"] = []
+        for dx in range(NX):
+            for other in range(2):
+                if dx == 0 and other == 0:
+                    continue
+                i = 2 * dx + other
+                xd = x_of(dx)
+                cd = core if other == 0 else 1 - core
+                st["out"].append(
+                    go(
+                        ob.at[g_rows(2 * xd + cd), :], ig_ref.at[:, own_cols],
+                        oxs.at[i], oxr.at[i], at(y, xd, cd, z),
+                    )
+                )
+        ig_ref[:, own_cols] = ob[g_rows(seat), :]
 
     st = {}
 
@@ -248,7 +272,6 @@
         ga[g_rows(seat), lanes(z)] = g_ref[g_rows(z), :]
         for c in loads[2:]:
             c.wait()
-        tick(0)
 
     def left():
         qs = st["qs"]
@@ -276,6 +299,7 @@
         c = go(pb.at[pl.ds(2 * (1 - core), 2)], pcr, cs.at[0], crs.at[0], sibling)
         w_forward(1)
         w_forward(2)
+        tick(0)
         got(c)
 
         @pl.loop(0, 8)
@@ -291,6 +315,8 @@
         g_share()
         w_share(1)
         w_share(2)
+        w_forward(3)
+        w_forward(4)
         for c in copies:
             got(c)
         total = ph[plane]
@@ -305,6 +331,9 @@
             zd = z_of(k)
             copies.append(go(zb.at[zd], pzr.at[k], zs.at[k], zr.at[k], (dp, zd)))
         tick(1)
+        w_share(3)
+        w_share(4)
+        w_relay(0)
         for c in copies:
             got(c)
         total = zb[z]
@@ -313,12 +342,14 @@
         zf[z] = total
         own = zf.at[z]
         copies = [go(own, own, zgs.at[k], zgr.at[k], (dp, z_of(k))) for k in range(1, NZ)]
-        w_forward(3)
-        w_forward(4)
+        w_forward(5)
+        w_forward(6)
         tick(2)
-        w_share(3)
-        w_share(4)
-        w_relay(0)
+        tick(3)
+        w_share(5)
+        w_share(6)
+        w_relay(1)
+        settle()
         for c in copies:
             got(c)
         pfin[core, plane] = jnp.concatenate([zf[r] for r in range(NZ)], axis=0)
@@ -328,19 +359,22 @@
         copies = []
         for k in range(1, NP):
             copies.append(go(own, own, ags.at[k], agr.at[k], (2 * p_of(k) + core, z)))
-        tick(3)
-        w_relay(1)
+        w_forward(7)
+        tick(4)
+        tick(5)
+        w_share(7)
+        w_relay(2)
         g_pass(0)
         g_pass(1)
-        w_forward(5)
-        w_forward(6)
+        w_relay(3)
+        settle()
         for c in copies:
             got(c)
         half = pfin.at[core]
         c = go(half, half, cs.at[1], crs.at[1], sibling)
-        w_share(5)
-        w_share(6)
-        tick(4)
+        tick(6)
+        g_pass(2)
+        w_relay(4)
         got(c)
 
     def right():
@@ -362,11 +396,9 @@
         st["gram"] = gram[:, 0:R] + gram[:, R : 2 * R] + gram[:, 2 * R : 3 * R]
         yb[...] = jnp.concatenate([yt[:16], yt[16:]], axis=1)
         copies = [go(yb, yr.at[k], ys.at[k], yrs.at[k], (dp, z_of(k))) for k in range(1, NZ)]
-        w_forward(7)
-        w_share(7)
-        tick(5)
-        w_relay(2)
-        w_relay(3)
+        tick(7)
+        for m in range(5, 8):
+            w_relay(m)
         qt = lax.fori_loop(
             0, 8, lambda cb, t: t + mm(ps[cb], f_ref[f_rows(cb), :], NN), jnp.zeros((96, 384), F32)
         )
@@ -375,7 +407,9 @@
         st["l"] = jnp.concatenate(
             [jnp.concatenate([part] * 3, axis=1) for part in split3(linv)], axis=0
         )
-        g_pass(2)
+        tick(8)
+        settle()
+        columns([0, 1, 2, 3])
         for c in copies:
             got(c)
         for k in range(1, NZ):
@@ -388,16 +422,14 @@
 
     def sum_right():
         c = go(qb.at[1 - core], qcr, cs.at[2], crs.at[2], sibling)
-        tick(6)
+        tick(9)
         got(c)
         own = qp.at[plane]
         own[...] = qb[core] + qcr[...]
         copies = []
         for k in range(1, NP):
             copies.append(go(own, own, qps.at[k], qpr_s.at[k], (2 * p_of(k) + core, z)))
-        tick(7)
-        w_relay(4)
-        w_relay(5)
+        tick(10)
         lparts = st["l"]
 
         @pl.loop(0, 8)
@@ -405,12 +437,15 @@
             hi, mid, low = split3(fold3(mm(lparts, ps[cb], NN)))
             pst[cb] = jnp.concatenate([hi, hi, hi, mid, mid, low], axis=0)
 
-        tick(8)
+        columns([4, 5, 6, 7])
+        send_columns()
+        tick(11)
 
         @pl.loop(0, 8)
         def _(cb):
             acc[cb] = merge(cb, [0, 1, 2])
 
+        settle()
         for c in copies:
             got(c)
         total = qp[0]
@@ -419,10 +454,13 @@
         own = qfin.at[core]
         own[...] = total
         c = go(own, own, cs.at[3], crs.at[3], sibling)
-        w_relay(6)
-        w_relay(7)
-        tick(9)
-        columns([0, 1, 2, 3])
+        tick(12)
+
+        @pl.loop(0, 8)
+        def _(cb):
+            acc[cb] = merge(cb, [3, 4])
+
+        settle()
         got(c)
         qall = stack3(jnp.concatenate([qfin[0], qfin[1]], axis=0))
         qn = fold3(mm(lparts, qall, NN)) * (1.0 / 32.0)
@@ -431,40 +469,17 @@
         qst[...] = jnp.concatenate([hi, mid, low, hi, mid, hi], axis=0)
 
     def finish():
-        tick(10)
-        columns([4, 5, 6, 7])
-        own_cols = pl.ds(pl.multiple_of(640 * seat, 128), 640)
-        out = []
-        for dx in range(NX):
-            for other in range(2):
-                if dx == 0 and other == 0:
-                    continue
-                i = 2 * dx + other
-                xd = x_of(dx)
-                cd = core if other == 0 else 1 - core
-                out.append(
-                    go(
-                        ob.at[g_rows(2 * xd + cd), :], ig_ref.at[:, own_cols],
-                        oxs.at[i], oxr.at[i], at(y, xd, cd, z),
-                    )
-                )
-        ig_ref[:, own_cols] = ob[g_rows(seat), :]
-        tick(11)
-
-        @pl.loop(0, 8)
-        def _(cb):
-            acc[cb] = merge(cb, [3, 4], factors=True)
-
-        for t in range(12, 16):
+        for t in range(13, 16):
             tick(t)
+        settle()
         for t in range(4):
             got(tl[12 + t])
 
             @pl.loop(2 * t, 2 * t + 2)
             def _(cb):
-                nf_ref[f_rows(cb), :] = merge(cb, [5, 6, 7]).astype(BF16)
-
-        for c in out:
+                nf_ref[f_rows(cb), :] = merge(cb, [5, 6, 7], factors=True).astype(BF16)
+
+        for c in st["out"]:
             got(c)
 
     steps = [
@@ -472,8 +487,8 @@
     ]
     for step in steps:
         step()
-    for c in sent:
-        c.wait_send()
+    settle()
+    settle()
 
 
 def store_kernel(a, b, c, a_out, b_out, c_out, sems):

time: 90.6 us -> 89.1 us (0.983)
  Pallas kernels: 89.9 us -> 88.4 us
    pallas_call x1, Pallas kernels: 87.7 us -> 86.3 us  [local(): pl.pallas_call(main_kernel, name='all_steps', out_shape=(jax.ShapeDtypeSt...]
where the time goes in v3:
time: 89.1 us
  Pallas kernels  88.4 us (99%)
    pallas_call x1, Pallas kernels, local(): pl.pallas_call(main_kernel, name='all_steps', out_shape=(jax.ShapeDtypeSt...  86.3 us
    pallas_call x1, Pallas kernels, local(): pl.pallas_call(store_kernel, name='store', out_shape=tuple((jax.ShapeDtyp...  2.17 us

profile of v3, /device:TPU:1, one launch (start us, length us, event | category | flops | bytes accessed | tf_op | source)
XLA Modules:
  0.0 89.1 jit_solution(17048210591891217019)
XLA Ops:
  0.6 86.3 %all_steps.1 = (bf16[64,5120]{1,0:T(8,128)(2,1)S(1)}, bf16[5120,384]{1,0:T(8,128)(2,1)S(1)}, f32[32,384]{1,0:T(8,128)S(1)}) custom-call(bf16[64,5120]{1,0:T(8,128)(2,1)} %x_hbm.1, bf16[512,384]{1,0:T(8,128)(2,1)} %g_hbm.1, f32[32,384]{1,0:T(8,128)} %bitcast.6, bf16[5120,384]{1,0:T(8,128)(2,1)} %w_hbm.1, bf16[5120,384]{1,0:T(8,128)(2,1)} %bitcast.4), custom_call_target="tpu_custom_call" | custom-call | flops 5000000000 | bytes 13000000 | tf_op jit(solution)/shard_map/all_steps/pallas_call | solution.py:510
  86.9 2.2 %store.1 = (bf16[64,5120]{1,0:T(8,128)(2,1)}, bf16[5120,384]{1,0:T(8,128)(2,1)}, f32[32,384]{1,0:T(8,128)}) custom-call(bf16[64,5120]{1,0:T(8,128)(2,1)S(1)} %get-tuple-element.9.a, bf16[5120,384]{1,0:T(8,128)(2,1)S(1)} %get-tuple-element.10.b, f32[32,384]{1,0:T(8,128)S(1)} %get-tuple-element.11.c), custom_call_target="tpu_custom_call" | custom-call | tf_op jit(solution)/shard_map/store/pallas_call | solution.py:573

commit v4 on v3

--- a/solution.py
+++ b/solution.py
@@ -397,8 +397,6 @@
         yb[...] = jnp.concatenate([yt[:16], yt[16:]], axis=1)
         copies = [go(yb, yr.at[k], ys.at[k], yrs.at[k], (dp, z_of(k))) for k in range(1, NZ)]
         tick(7)
-        for m in range(5, 8):
-            w_relay(m)
         qt = lax.fori_loop(
             0, 8, lambda cb, t: t + mm(ps[cb], f_ref[f_rows(cb), :], NN), jnp.zeros((96, 384), F32)
         )
@@ -407,6 +405,8 @@
         st["l"] = jnp.concatenate(
             [jnp.concatenate([part] * 3, axis=1) for part in split3(linv)], axis=0
         )
+        for m in range(5, 8):
+            w_relay(m)
         tick(8)
         settle()
         columns([0, 1, 2, 3])

time: 89.1 us -> 89.1 us (level)
  no operation moved by 1% of the time
where the time goes in v4:
time: 89.1 us
  Pallas kernels  88.4 us (99%)
    pallas_call x1, Pallas kernels, local(): pl.pallas_call(main_kernel, name='all_steps', out_shape=(jax.ShapeDtypeSt...  86.3 us
    pallas_call x1, Pallas kernels, local(): pl.pallas_call(store_kernel, name='store', out_shape=tuple((jax.ShapeDtyp...  2.17 us

profile of v4, /device:TPU:1, one launch (start us, length us, event | category | flops | bytes accessed | tf_op | source)
XLA Modules:
  0.0 89.1 jit_solution(12366516733767091345)
XLA Ops:
  0.6 86.3 %all_steps.1 = (bf16[64,5120]{1,0:T(8,128)(2,1)S(1)}, bf16[5120,384]{1,0:T(8,128)(2,1)S(1)}, f32[32,384]{1,0:T(8,128)S(1)}) custom-call(bf16[64,5120]{1,0:T(8,128)(2,1)} %x_hbm.1, bf16[512,384]{1,0:T(8,128)(2,1)} %g_hbm.1, f32[32,384]{1,0:T(8,128)} %bitcast.6, bf16[5120,384]{1,0:T(8,128)(2,1)} %w_hbm.1, bf16[5120,384]{1,0:T(8,128)(2,1)} %bitcast.4), custom_call_target="tpu_custom_call" | custom-call | flops 5000000000 | bytes 13000000 | tf_op jit(solution)/shard_map/all_steps/pallas_call | solution.py:510
  86.9 2.2 %store.1 = (bf16[64,5120]{1,0:T(8,128)(2,1)}, bf16[5120,384]{1,0:T(8,128)(2,1)}, f32[32,384]{1,0:T(8,128)}) custom-call(bf16[64,5120]{1,0:T(8,128)(2,1)S(1)} %get-tuple-element.9.a, bf16[5120,384]{1,0:T(8,128)(2,1)S(1)} %get-tuple-element.10.b, f32[32,384]{1,0:T(8,128)S(1)} %get-tuple-element.11.c), custom_call_target="tpu_custom_call" | custom-call | tf_op jit(solution)/shard_map/store/pallas_call | solution.py:573
